TPU v7x, 768 devices: a whole 4x8x12 slice. The times are simulated.
768 devices in a mesh: dp: 128 (over z_lo, x, y), tensor: 6 (over z_hi, core).
Axes of the slice: x: 4, y: 8, z: 12 (z_hi: 3, z_lo: 4; z = z_hi * 4 + z_lo), core: 2. Of those that a mesh axis runs over, the one named last changes fastest.
Arguments:
- inputs: bfloat16 [2048, 6144], P('dp', 'tensor'), may hold values from -6 to 6
- in_basis: bfloat16 [48, 128, 128], P('tensor'), may hold values from -0.5 to 0.5
- out_grads: bfloat16 [2048, 6144], P('dp', 'tensor'), may hold values from -6 to 6
- out_basis: bfloat16 [6144, 6144], P('tensor', 'dp'), may hold values from -0.078125 to 0.078125
Outputs:
- eigen_values: float32 [6144, 6144], P('tensor', 'dp')
All inputs are finite; a program needn't handle non-finite values.
Results may differ from a plain program's by a relative error of at most 0.00041.
Values may be sent and summed in bfloat16 or wider, within the bound.
A program may use at most 32 MiB of HBM per device.

v0:
```python
import jax
import jax.numpy as jnp
from jax import lax
from jax.sharding import PartitionSpec as P


def rotate_heads(inputs, in_basis):
    token_count = inputs.shape[0]
    head_count = in_basis.shape[0]
    head_size = in_basis.shape[1]
    split_heads = inputs.reshape(token_count, head_count, head_size)
    rotated = jnp.einsum("thd,hde->the", split_heads, in_basis, preferred_element_type=jnp.float32)
    rotated = rotated.reshape(token_count, head_count * head_size)
    return (rotated * rotated).astype(jnp.bfloat16)


def squared_sum(partial_value):
    summed = lax.psum(partial_value, "tensor")
    return (summed * summed).astype(jnp.bfloat16)


def transposed_product(left, right):
    return lax.dot_general(
        left, right, (((0,), (0,)), ((), ())), preferred_element_type=jnp.float32
    )


def per_device(inputs, in_basis, out_grads, out_basis):
    square_in = rotate_heads(inputs, in_basis)
    partial_value = jnp.dot(
        lax.all_gather(out_grads, "dp", axis=0, tiled=True),
        out_basis,
        preferred_element_type=jnp.float32,
    )
    square_out = squared_sum(partial_value)
    eigen_tile = transposed_product(lax.all_gather(square_in, "dp", axis=0, tiled=True), square_out)
    return eigen_tile / jnp.float32(square_out.shape[0])


def solution(mesh):
    in_specs = (P("dp", "tensor"), P("tensor", None, None), P("dp", "tensor"), P("tensor", "dp"))
    out_specs = P("tensor", "dp")
    return jax.shard_map(
        per_device, mesh=mesh, in_specs=in_specs, out_specs=out_specs, check_vma=False
    )
```

profile of v0, /device:TPU:1, one launch (start us, length us, event | category | flops | bytes accessed | tf_op | source)
XLA Modules:
  0.0 1510.5 jit_solution(2321681263396959793)
XLA Ops:
  6.5 0.0 copy-start
  6.5 0.0 all-gather.5.cloned.1.call-start
  6.5 0.7 all-gather.5.cloned.1.call-update
  7.3 0.0 all-gather.3.cloned.1.call-start
  7.3 0.2 copy-done
  7.5 0.9 fusion.1
  8.4 0.6 copy.15
  9.0 0.0 all-gather.3.cloned.1.call-update
  9.1 0.0 all-reduce.2.cloned.1.call-start
  9.1 617.1 %all-gather.5.cloned.1.call-done = bf16[2048,1024]{1,0:T(8,128)(2,1)} async-done(((bf16[16,1024]{1,0:T(8,128)(2,1)}), bf16[2048,1024]{1,0:T(8,128)(2,1)}) %all-gather.5.cloned.1.call-update) | async-done | bytes 4194320 | tf_op jit(solution)/shard_map/all_gather | solution.py:31
  626.2 4.5 fusion.4
  630.7 0.0 all-reduce.2.cloned.1.call-update
  630.7 689.1 %all-gather.3.cloned.1.call-done = bf16[2048,1024]{1,0:T(8,128)(2,1)} async-done(((bf16[16,1024]{1,0:T(8,128)(2,1)}), bf16[2048,1024]{1,0:T(8,128)(2,1)}) %all-gather.3.cloned.1.call-update) | async-done | bytes 4194320 | tf_op jit(solution)/shard_map/all_gather | solution.py:36
  1319.9 180.0 %all-reduce.2.cloned.1.call-done = f32[2048,48]{1,0:T(8,128)} async-done(((f32[2048,48]{1,0:T(8,128)}), f32[2048,48]{1,0:T(8,128)}) %all-reduce.2.cloned.1.call-update) | async-done | bytes 393232 | tf_op jit(solution)/shard_map/psum | solution.py:18
  1499.9 4.0 convolution_multiply_fusion
Async XLA Ops:
  6.5 1.0 copy-start
  6.5 619.7 %all-gather.5.cloned.1.call-start = ((), (), s32[]{:S(2)}) async-start(), calls=%async_computation.1 | async-start | bytes 4227072 | tf_op jit(solution)/shard_map/all_gather | solution.py:31
  7.3 1312.6 %all-gather.3.cloned.1.call-start = ((), (), s32[]{:S(2)}) async-start(), calls=%async_computation | async-start | bytes 4227072 | tf_op jit(solution)/shard_map/all_gather | solution.py:36
  9.1 1490.8 %all-reduce.2.cloned.1.call-start = ((), (), s32[]{:S(2)}) async-start(), calls=%async_computation.2 | async-start | bytes 2097152 | tf_op jit(solution)/shard_map/psum | solution.py:18
Sparse Core Ops, SparseCore 0:
  9.7 616.4 all-gather.4
  628.6 691.2 all-gather.2
  1323.1 176.7 all-reduce.1
where the time goes:
time: 1510 us
  waiting for transfers between devices  1490 us (99%)
    all_gather x1, waiting for transfers between devices, per_device(): lax.all_gather(square_in, 'dp', axis=0, tiled=True)  689 us
    all_gather x1, waiting for transfers between devices, per_device(): lax.all_gather(out_grads, 'dp', axis=0, tiled=True)  617 us
    psum x1, waiting for transfers between devices, squared_sum(): summed = lax.psum(partial_value, 'tensor')  180 us
  transfers between devices with their start and end apart: 3, of which 3 were waited for; matrix products, arithmetic and copies ran while one was open for 0% of the time, Pallas kernels for 0%

commit v1 on v0

v1 whole, which is shorter than its diff:
```python
import jax
import jax.numpy as jnp
from jax import lax
from jax.experimental import pallas as pl
from jax.experimental.pallas import tpu as pltpu
from jax.sharding import PartitionSpec as P

MESH = pl.DeviceIdType.MESH
BF16, F32 = jnp.bfloat16, jnp.float32
NZ, NX, NY, NH, NC = 4, 4, 8, 3, 2
NT = NH * NC
TOK, FEAT, COLS = 16, 1024, 48
HEADS, HD = 8, 128
TOKENS = 2048
SLICE = NX * COLS // NT
HALF = NY * NZ * TOK // 2
ZORDER = (0, 1, 3, 2)


def place(r):
    return (r + 2) % NY


def kernel(
    inp, basis, grad, ob, out,
    gbuf, sbuf, bbuf, inp_v, basis_v, part, part_in, sq, eig, eig_in,
    lsem, gsend, grecv, ssend, srecv, bsend, brecv, psend, precv, qsend, qrecv, esend, erecv,
):
    dp, tensor = lax.axis_index("dp"), lax.axis_index("tensor")
    zl, x, y = dp // (NX * NY), (dp // NY) % NX, dp % NY
    zh, core = tensor // NC, tensor % NC

    def at_dp(z_, x_, y_):
        return ((z_ % NZ) * NX * NY + (x_ % NX) * NY + y_ % NY, tensor)

    zpeer = {k: at_dp(zl + k, x, y) for k in range(1, NZ)}
    xpeer = {k: at_dp(zl, x + k, y) for k in range(1, NX)}
    ypeer = {1: at_dp(zl, x, y + 1), -1: at_dp(zl, x, y + NY - 1)}
    toff = [(a, b) for a in range(NH) for b in range(NC) if a or b]
    tidx = [((zh + a) % NH) * NC + (core + b) % NC for a, b in toff]
    tpeer = [(dp, t) for t in tidx]
    tback = [toff.index(((NH - a) % NH, b)) for a, b in toff]

    peers = list(zpeer.values()) + list(xpeer.values()) + list(ypeer.values()) + tpeer
    barrier = pltpu.get_barrier_semaphore()
    for p in peers:
        pl.semaphore_signal(barrier, inc=1, device_id=p, device_id_type=MESH)

    local = [
        pltpu.make_async_copy(inp, inp_v, lsem.at[0]),
        pltpu.make_async_copy(basis, basis_v, lsem.at[1]),
        pltpu.make_async_copy(grad, gbuf.at[place(0), 0], lsem.at[2]),
        pltpu.make_async_copy(ob, bbuf.at[0], lsem.at[3]),
    ]
    for c in local:
        c.start()
    pl.semaphore_wait(barrier, len(peers))

    sends = []

    def send(src, dst, ss, rs, dev):
        c = pltpu.make_async_remote_copy(
            src_ref=src, dst_ref=dst, send_sem=ss, recv_sem=rs, device_id=dev, device_id_type=MESH
        )
        c.start()
        sends.append(c)

    def landed(ref, sem):
        pltpu.make_async_copy(ref, ref, sem).wait()

    def spread(buf, ss, rs, own):
        for k in (1, 3, 2):
            zr = (NZ - k) % NZ
            send(own, buf.at[place(0), zr], ss.at[0, zr], rs.at[0, zr], zpeer[k])

    def hop(buf, ss, rs, d, own=None):
        up, down = d, (NY - d) % NY
        for i, zr in enumerate(ZORDER):
            if d == 0 and zr:
                landed(buf.at[place(0), zr], rs.at[0, zr])
            if d:
                landed(buf.at[place(up), zr], rs.at[up, zr])
            if d < 3 or i < 2:
                src = own if d == 0 and zr == 0 else buf.at[place(up), zr]
                send(src, buf.at[place(up + 1), zr], ss.at[up + 1, zr], rs.at[up + 1, zr], ypeer[1])
            if d:
                landed(buf.at[place(down), zr], rs.at[down, zr])
            if d < 3 or i >= 2:
                src = own if d == 0 and zr == 0 else buf.at[place(down), zr]
                to = (down - 1) % NY
                send(src, buf.at[place(to), zr], ss.at[to, zr], rs.at[to, zr], ypeer[-1])

    def last(buf, rs):
        for zr in ZORDER:
            landed(buf.at[place(4), zr], rs.at[4, zr])

    spread(gbuf, gsend, grecv, grad)
    for k in (1, 3, 2):
        to = NX - k
        send(ob, bbuf.at[to], bsend.at[to - 1], brecv.at[to - 1], xpeer[k])
    local[0].wait()
    local[1].wait()
    mine = sbuf.at[place(0), 0]
    for h in range(HEADS):
        cut = slice(h * HD, (h + 1) * HD)
        rot = jnp.dot(inp_v[:, cut], basis_v[h], preferred_element_type=F32)
        mine[:, cut] = (rot * rot).astype(BF16)
    hop(gbuf, gsend, grecv, 0, grad)
    spread(sbuf, ssend, srecv, mine)
    hop(gbuf, gsend, grecv, 1)
    hop(sbuf, ssend, srecv, 0, mine)
    hop(gbuf, gsend, grecv, 2)

    local[2].wait()
    local[3].wait()
    for k in range(1, NX):
        landed(bbuf.at[k], brecv.at[k - 1])

    def partial(h):
        lhs = bbuf[...].reshape(NX * COLS, FEAT)
        rhs = gbuf[4 * h : 4 * h + 4].reshape(HALF, FEAT)
        p = lax.dot_general(lhs, rhs, (((1,), (1,)), ((), ())), preferred_element_type=F32)
        part[h] = p.reshape(NT, SLICE, HALF)
        for k in range(NT - 1):
            send(
                part.at[h, tidx[k]], part_in.at[h, tback[k]],
                psend.at[h, k], precv.at[h, tback[k]], tpeer[k],
            )

    def total(h):
        acc = part[h, tensor]
        for k in range(NT - 1):
            landed(part_in.at[h, k], precv.at[h, k])
            acc = acc + part_in[h, k]
        sq[h, tensor] = (acc * acc).astype(BF16)
        for k in range(NT - 1):
            send(
                sq.at[h, tensor], sq.at[h, tensor],
                qsend.at[h, k], qrecv.at[h, tback[k]], tpeer[k],
            )

    partial(0)
    hop(sbuf, ssend, srecv, 1)
    hop(gbuf, gsend, grecv, 3)
    hop(sbuf, ssend, srecv, 2)
    last(gbuf, grecv)
    partial(1)
    total(0)
    hop(sbuf, ssend, srecv, 3)
    total(1)
    last(sbuf, srecv)
    for h in range(2):
        for k in range(NT - 1):
            landed(sq.at[h, tidx[k]], qrecv.at[h, k])
    for k in (2, 1, 3, 0):
        acc = None
        for h in range(2):
            lhs = sq[h].reshape(NX * COLS, HALF)[k * COLS : (k + 1) * COLS]
            rhs = sbuf[4 * h : 4 * h + 4].reshape(HALF, FEAT)
            p = jnp.dot(lhs, rhs, preferred_element_type=F32)
            acc = p if acc is None else acc + p
        eig[k] = acc
        if k:
            to = NX - k
            send(eig.at[k], eig_in.at[to - 1], esend.at[to - 1], erecv.at[to - 1], xpeer[k])
    acc = eig[0]
    for k in (1, 3, 2):
        landed(eig_in.at[k - 1], erecv.at[k - 1])
        acc = acc + eig_in[k - 1]
    out[...] = acc * F32(1.0 / TOKENS)
    for c in sends:
        c.wait_send()


def per_device(inputs, in_basis, out_grads, out_basis):
    dma = pltpu.SemaphoreType.DMA
    hbm = pl.BlockSpec(memory_space=pl.ANY)
    eigen = pl.pallas_call(
        kernel,
        out_shape=jax.ShapeDtypeStruct((COLS, FEAT), F32),
        in_specs=[hbm] * 4,
        out_specs=pl.BlockSpec(memory_space=pltpu.VMEM),
        scratch_shapes=[
            pltpu.VMEM((NY, NZ, TOK, FEAT), BF16),
            pltpu.VMEM((NY, NZ, TOK, FEAT), BF16),
            pltpu.VMEM((NX, COLS, FEAT), BF16),
            pltpu.VMEM((TOK, FEAT), BF16),
            pltpu.VMEM((HEADS, HD, HD), BF16),
            pltpu.VMEM((2, NT, SLICE, HALF), F32),
            pltpu.VMEM((2, NT - 1, SLICE, HALF), F32),
            pltpu.VMEM((2, NT, SLICE, HALF), BF16),
            pltpu.VMEM((NX, COLS, FEAT), F32),
            pltpu.VMEM((NX - 1, COLS, FEAT), F32),
            dma((4,)),
            dma((NY, NZ)), dma((NY, NZ)),
            dma((NY, NZ)), dma((NY, NZ)),
            dma((NX - 1,)), dma((NX - 1,)),
            dma((2, NT - 1)), dma((2, NT - 1)),
            dma((2, NT - 1)), dma((2, NT - 1)),
            dma((NX - 1,)), dma((NX - 1,)),
        ],
        compiler_params=pltpu.CompilerParams(
            collective_id=0, has_side_effects=True, vmem_limit_bytes=60 << 20
        ),
        cost_estimate=pl.CostEstimate(flops=4 * 10**8, bytes_accessed=10**6, transcendentals=0),
        name="eigen_fit",
    )(inputs, in_basis, out_grads, out_basis.T)
    return eigen.T


def solution(mesh):
    in_specs = (P("dp", "tensor"), P("tensor", None, None), P("dp", "tensor"), P("tensor", "dp"))
    out_specs = P("tensor", "dp")
    return jax.shard_map(
        per_device, mesh=mesh, in_specs=in_specs, out_specs=out_specs, check_vma=False
    )
```

time: 1510 us -> 70.3 us (0.05)
  waiting for transfers between devices: 1490 us -> 0 us
  Pallas kernels: 0 us -> 68.5 us
    all_gather x2 -> x0, waiting for transfers between devices: 1310 us -> none  [the longest x1 689 us: per_device(): lax.all_gather(square_in, 'dp', axis=0, tiled=True)]
    psum x1 -> x0, waiting for transfers between devices: 180 us -> none  [squared_sum(): summed = lax.psum(partial_value, 'tensor')]
    pallas_call x0 -> x1, Pallas kernels: none -> 68.5 us  [per_device(): pl.pallas_call(kernel, out_shape=jax.ShapeDtypeStruct((COLS, FEAT), F32),...]
  transfers between devices with their start and end apart: 3 -> 0, of which waited for: 3 -> 0; matrix products, arithmetic and copies ran while one was open for 0% -> 0% of each run, Pallas kernels for 0% -> 0%
where the time goes in v1:
time: 70.3 us; the launch traced here: 70.1 us
  Pallas kernels  68.5 us (97%)
  local copies, waits for them, and re-layouts  1.62 us (2%)
    pallas_call x1, Pallas kernels, per_device(): pl.pallas_call(kernel, out_shape=jax.ShapeDtypeStruct((COLS, FEAT), F32),...  68.5 us
    unnamed x1, local copies, waits for them, and re-layouts  1.62 us

profile of v1, /device:TPU:1, one launch (start us, length us, event | category | flops | bytes accessed | tf_op | source)
XLA Modules:
  0.0 70.1 jit_solution(7062942592801836110)
XLA Ops:
  0.0 68.5 %eigen_fit.1 = f32[48,1024]{1,0:T(8,128)} custom-call(bf16[16,1024]{1,0:T(8,128)(2,1)} %inp.1, bf16[8,128,128]{2,1,0:T(8,128)(2,1)} %basis.1, bf16[16,1024]{1,0:T(8,128)(2,1)} %grad.1, bf16[48,1024]{1,0:T(8,128)(2,1)} %bitcast.3), custom_call_target="tpu_custom_call" | custom-call | flops 400000000 | bytes 1000000 | tf_op jit(solution)/shard_map/eigen_fit/pallas_call | solution.py:178
  68.5 1.6 %copy.6 = f32[1024,48]{0,1:T(8,128)} copy(f32[1024,48]{0,1:T(8,128)} %bitcast.2) | data formatting | bytes 393216

commit v2 on v0

v2 whole, which is shorter than its diff:
```python
import jax
import jax.numpy as jnp
from jax import lax
from jax.experimental import pallas as pl
from jax.experimental.pallas import tpu as pltpu
from jax.sharding import PartitionSpec as P

MESH = pl.DeviceIdType.MESH
BF16, F32 = jnp.bfloat16, jnp.float32
NZ, NX, NY, NH, NC = 4, 4, 8, 3, 2
NT = NH * NC
NQ = 2
NP = NY // NQ
TOK, FEAT, COLS = 16, 1024, 48
FH = FEAT // 2
HEADS, HD = 8, 128
TOKENS = 2048
PTOK = NP * NZ * TOK
SLICE = NX * COLS // NT
SENDS = 128


def kernel(
    inp, basis, grad, ob, out,
    ga, gb, sbuf, bbuf, inp_v, basis_v, part, sib_in, psum, zin, away, sq, eig, eig_in,
    lsem, ssem, garecv, gbrecv, srecv, brecv, crecv, zrecv, qrecv, erecv,
):
    dp, tensor = lax.axis_index("dp"), lax.axis_index("tensor")
    zl, x, y = dp // (NX * NY), (dp // NY) % NX, dp % NY
    zh, core = tensor // NC, tensor % NC
    par, yh = y % NQ, y // NQ
    ymate = y + 1 - 2 * par

    def device(z_, x_, y_, h_=None):
        place = (z_ % NZ) * NX * NY + (x_ % NX) * NY + y_ % NY
        return (place, tensor if h_ is None else (h_ % NH) * NC + core)

    zpeer = [device(zl + k, x, y) for k in (1, 3, 2)]
    xpeer = {k: device(zl, x + k, y) for k in (2, 1, 3)}
    yfar = [device(zl, x, y + k) for k in (2, 6, 4)]
    yup, ydown = device(zl, x, y + 1), device(zl, x, y + NY - 1)
    mate = [device(zl, x, ymate, zh + a) for a in range(NH)]
    hpeer = [device(zl, x, y, zh + a) for a in (1, 2)]
    twin = (dp, zh * NC + 1 - core)

    peers = zpeer + list(xpeer.values()) + yfar + [yup, ydown] + mate[1:] + hpeer + [twin]
    barrier = pltpu.get_barrier_semaphore()
    for p in peers:
        pl.semaphore_signal(barrier, inc=1, device_id=p, device_id_type=MESH)

    lo, hi = pl.ds(0, FH), pl.ds(FH, FH)
    local = [
        pltpu.make_async_copy(inp, inp_v, lsem.at[0]),
        pltpu.make_async_copy(basis, basis_v, lsem.at[1]),
        pltpu.make_async_copy(grad.at[:, lo], ga.at[yh, zl], lsem.at[2]),
        pltpu.make_async_copy(grad.at[:, hi], gb.at[yh, zl], lsem.at[3]),
        pltpu.make_async_copy(ob, bbuf.at[par, 0], lsem.at[4]),
    ]
    for c in local:
        c.start()
    pl.semaphore_wait(barrier, len(peers))

    sends = []

    def send(src, dst, rs, dev):
        c = pltpu.make_async_remote_copy(
            src_ref=src, dst_ref=dst, send_sem=ssem.at[len(sends)], recv_sem=rs,
            device_id=dev, device_id_type=MESH,
        )
        c.start()
        sends.append(c)

    def landed(ref, sem):
        pltpu.make_async_copy(ref, ref, sem).wait()

    for d in zpeer:
        send(grad.at[:, lo], ga.at[yh, zl], garecv.at[yh, zl], d)
    for d in yfar:
        send(grad.at[:, hi], gb.at[yh, zl], gbrecv.at[yh, zl], d)
    send(ob, bbuf.at[par, 0], brecv.at[par, 0], mate[0])
    for d in yfar:
        send(grad.at[:, lo], ga.at[yh, zl], garecv.at[yh, zl], d)
    for d in zpeer:
        send(grad.at[:, hi], gb.at[yh, zl], gbrecv.at[yh, zl], d)
    for k, d in xpeer.items():
        send(ob, bbuf.at[par, NX - k], brecv.at[par, NX - k], d)

    local[0].wait()
    local[1].wait()
    mine = sbuf.at[par, yh, zl]
    for h in range(HEADS):
        cut = slice(h * HD, (h + 1) * HD)
        rot = jnp.dot(inp_v[:, cut], basis_v[h], preferred_element_type=F32)
        mine[:, cut] = (rot * rot).astype(BF16)

    def slot(y_, z_):
        return sbuf.at[y_ % NQ, y_ // NQ, z_], srecv.at[y_, z_]

    zs = [(zl + k) % NZ for k in (0, 1, 3, 2)]

    def hop(d, zz=None):
        up, down = (y + NY - d) % NY, (y + d) % NY
        for i, z_ in enumerate(zs):
            if zz is not None and not any(z_ is w for w in zz):
                continue
            if d or i:
                landed(*slot(up, z_))
            if d < 3 or i < 2:
                ref, sem = slot(up, z_)
                send(ref, ref, sem, yup)
            if d:
                landed(*slot(down, z_))
            if d < 3 or i >= 2:
                ref, sem = slot(down, z_)
                send(ref, ref, sem, ydown)

    for d in zpeer:
        ref, sem = slot(y, zl)
        send(ref, ref, sem, d)
    hop(0, zs[:1])

    for z_ in zs[1:]:
        landed(ga.at[yh, z_], garecv.at[yh, z_])
        for d in yfar:
            send(ga.at[yh, z_], ga.at[yh, z_], garecv.at[yh, z_], d)
    hs = [(yh + k) % NP for k in (0, 1, 3, 2)]
    for h_ in hs[1:]:
        landed(gb.at[h_, zl], gbrecv.at[h_, zl])
        for d in zpeer:
            send(gb.at[h_, zl], gb.at[h_, zl], gbrecv.at[h_, zl], d)
    other = 1 - par
    landed(bbuf.at[other, 0], brecv.at[other, 0])
    for k, d in xpeer.items():
        send(bbuf.at[other, 0], bbuf.at[other, NX - k], brecv.at[other, NX - k], d)

    hop(0, zs[1:])
    hop(1)
    local[2].wait()
    local[3].wait()
    local[4].wait()
    for h_ in hs[1:]:
        for z_ in zs:
            landed(ga.at[h_, z_], garecv.at[h_, z_])
    for z_ in zs[1:]:
        for h_ in hs:
            landed(gb.at[h_, z_], gbrecv.at[h_, z_])

    for q in (other, par):
        for k in (1, 3, 2):
            landed(bbuf.at[q, k], brecv.at[q, k])
        nt = (((1,), (1,)), ((), ()))
        lhs = bbuf[q].reshape(NX * COLS, FEAT)
        p = lax.dot_general(lhs[:, :FH], ga[...].reshape(PTOK, FH), nt, preferred_element_type=F32)
        p = p + lax.dot_general(lhs[:, FH:], gb[...].reshape(PTOK, FH), nt, preferred_element_type=F32)
        p = p.reshape(NH, NC, SLICE, PTOK)
        for c in range(NC):
            part[c, q] = p[:, c]
        send(part.at[1 - core, q], sib_in.at[q], crecv.at[q], twin)
    for q in (other, par):
        landed(sib_in.at[q], crecv.at[q])
        psum[q] = part[core, q] + sib_in[q]
        for i, d in enumerate(hpeer):
            send(psum.at[q, (zh + 1 + i) % NH], zin.at[q, 1 - i], zrecv.at[q, 1 - i], d)
    hop(2)
    for q in (other, par):
        acc = psum[q, zh]
        for i in range(NH - 1):
            landed(zin.at[q, i], zrecv.at[q, i])
            acc = acc + zin[q, i]
        val = (acc * acc).astype(BF16)
        if q is other:
            away[...] = val
            for d in mate:
                send(away, sq.at[par, tensor], qrecv.at[par, tensor], d)
        else:
            sq[par, tensor] = val
            for d in hpeer + [twin]:
                send(sq.at[par, tensor], sq.at[par, tensor], qrecv.at[par, tensor], d)
    hop(3)
    same = [((zh + a) % NH) * NC + core for a in range(NH)]
    across = [((zh + a) % NH) * NC + 1 - core for a in range(NH)]
    for q, js in ((other, same), (par, same[1:])):
        for j in js:
            landed(sq.at[q, j], qrecv.at[q, j])
            send(sq.at[q, j], sq.at[q, j], qrecv.at[q, j], twin)
    for z_ in zs:
        landed(*slot((y + 4) % NY, z_))
    for q in (other, par):
        for j in across:
            landed(sq.at[q, j], qrecv.at[q, j])

    for n in range(2):
        acc = None
        for q in range(NQ):
            rhs = sbuf[q, :, :, :, n * FH : (n + 1) * FH].reshape(PTOK, FH)
            p = jnp.dot(sq[q].reshape(NX * COLS, PTOK), rhs, preferred_element_type=F32)
            acc = p if acc is None else acc + p
        eig[n] = acc.reshape(NX, COLS, FH)
        for k, d in xpeer.items():
            send(eig.at[n, k], eig_in.at[n, NX - k - 1], erecv.at[n, NX - k - 1], d)
    for n in range(2):
        acc = eig[n, 0]
        for k in (0, 2, 1):
            landed(eig_in.at[n, k], erecv.at[n, k])
            acc = acc + eig_in[n, k]
        out[:, n * FH : (n + 1) * FH] = acc * F32(1.0 / TOKENS)
    for c in sends:
        c.wait_send()


def per_device(inputs, in_basis, out_grads, out_basis):
    dma = pltpu.SemaphoreType.DMA
    hbm = pl.BlockSpec(memory_space=pltpu.HBM)
    eigen = pl.pallas_call(
        kernel,
        out_shape=jax.ShapeDtypeStruct((COLS, FEAT), F32),
        in_specs=[hbm] * 4,
        out_specs=pl.BlockSpec(memory_space=pltpu.VMEM),
        scratch_shapes=[
            pltpu.VMEM((NP, NZ, TOK, FH), BF16),
            pltpu.VMEM((NP, NZ, TOK, FH), BF16),
            pltpu.VMEM((NQ, NP, NZ, TOK, FEAT), BF16),
            pltpu.VMEM((NQ, NX, COLS, FEAT), BF16),
            pltpu.VMEM((TOK, FEAT), BF16),
            pltpu.VMEM((HEADS, HD, HD), BF16),
            pltpu.VMEM((NC, NQ, NH, SLICE, PTOK), F32),
            pltpu.VMEM((NQ, NH, SLICE, PTOK), F32),
            pltpu.VMEM((NQ, NH, SLICE, PTOK), F32),
            pltpu.VMEM((NQ, NH - 1, SLICE, PTOK), F32),
            pltpu.VMEM((SLICE, PTOK), BF16),
            pltpu.VMEM((NQ, NT, SLICE, PTOK), BF16),
            pltpu.VMEM((2, NX, COLS, FH), F32),
            pltpu.VMEM((2, NX - 1, COLS, FH), F32),
            dma((5,)),
            dma((SENDS,)),
            dma((NP, NZ)),
            dma((NP, NZ)),
            dma((NY, NZ)),
            dma((NQ, NX)),
            dma((NQ,)),
            dma((NQ, NH - 1)),
            dma((NQ, NT)),
            dma((2, NX - 1)),
        ],
        compiler_params=pltpu.CompilerParams(
            collective_id=0, has_side_effects=True, vmem_limit_bytes=24 << 20
        ),
        cost_estimate=pl.CostEstimate(flops=4 * 10**8, bytes_accessed=10**6, transcendentals=0),
        name="eigen_fit",
    )(*(pltpu.with_memory_space_constraint(a, pltpu.HBM) for a in (inputs, in_basis, out_grads, out_basis.T)))
    return eigen.T


def solution(mesh):
    in_specs = (P("dp", "tensor"), P("tensor", None, None), P("dp", "tensor"), P("tensor", "dp"))
    out_specs = P("tensor", "dp")
    return jax.shard_map(
        per_device, mesh=mesh, in_specs=in_specs, out_specs=out_specs, check_vma=False
    )
```

time: 1510 us -> 63.1 us (0.04)
  waiting for transfers between devices: 1490 us -> 0 us
  Pallas kernels: 0 us -> 62.2 us
    all_gather x2 -> x0, waiting for transfers between devices: 1310 us -> none  [the longest x1 689 us: per_device(): lax.all_gather(square_in, 'dp', axis=0, tiled=True)]
    psum x1 -> x0, waiting for transfers between devices: 180 us -> none  [squared_sum(): summed = lax.psum(partial_value, 'tensor')]
    pallas_call x0 -> x1, Pallas kernels: none -> 62.2 us  [per_device(): pl.pallas_call(kernel, out_shape=jax.ShapeDtypeStruct((COLS, FEAT), F32),...]
  transfers between devices with their start and end apart: 3 -> 0, of which waited for: 3 -> 0; matrix products, arithmetic and copies ran while one was open for 0% -> 0% of each run, Pallas kernels for 0% -> 0%
where the time goes in v2:
time: 63.1 us; the launch traced here: 62.9 us
  Pallas kernels  62.2 us (99%)
  local copies, waits for them, and re-layouts  0.68 us (1%)
    pallas_call x1, Pallas kernels, per_device(): pl.pallas_call(kernel, out_shape=jax.ShapeDtypeStruct((COLS, FEAT), F32),...  62.2 us

profile of v2, /device:TPU:1, one launch (start us, length us, event | category | flops | bytes accessed | tf_op | source)
XLA Modules:
  0.0 62.9 jit_solution(5096690711145862609)
XLA Ops:
  0.0 62.2 %eigen_fit.1 = f32[48,1024]{1,0:T(8,128)S(1)} custom-call(bf16[16,1024]{1,0:T(8,128)(2,1)} %inp.1, bf16[8,128,128]{2,1,0:T(8,128)(2,1)} %basis.1, bf16[16,1024]{1,0:T(8,128)(2,1)} %grad.1, bf16[48,1024]{1,0:T(8,128)(2,1)} %bitcast.3), custom_call_target="tpu_custom_call" | custom-call | flops 400000000 | bytes 1000000 | tf_op jit(solution)/shard_map/eigen_fit/pallas_call | solution.py:214
  62.3 0.7 %copy.6 = f32[1024,48]{0,1:T(8,128)} copy(f32[1024,48]{0,1:T(8,128)S(1)} %bitcast.2) | data formatting | bytes 393216

commit v3 on v2

--- a/solution.py
+++ b/solution.py
@@ -16,14 +16,16 @@
 HEADS, HD = 8, 128
 TOKENS = 2048
 PTOK = NP * NZ * TOK
-SLICE = NX * COLS // NT
-SENDS = 128
+NA = 2
+SLICE = NX * COLS // NT // NA
+SENDS = 160
+XSLOT = (1, 2, 0, 3)
 
 
 def kernel(
     inp, basis, grad, ob, out,
-    ga, gb, sbuf, bbuf, inp_v, basis_v, part, sib_in, psum, zin, away, sq, eig, eig_in,
-    lsem, ssem, garecv, gbrecv, srecv, brecv, crecv, zrecv, qrecv, erecv,
+    ga, gb, sbuf, bbuf, inp_v, basis_v, part, sib_in, psum, zin, away, sq, eig, eig_in, passing,
+    lsem, ssem, garecv, gbrecv, srecv, brecv, crecv, zrecv, qrecv, erecv, precv,
 ):
     dp, tensor = lax.axis_index("dp"), lax.axis_index("tensor")
     zl, x, y = dp // (NX * NY), (dp // NY) % NX, dp % NY
@@ -35,9 +37,9 @@
         place = (z_ % NZ) * NX * NY + (x_ % NX) * NY + y_ % NY
         return (place, tensor if h_ is None else (h_ % NH) * NC + core)
 
-    zpeer = [device(zl + k, x, y) for k in (1, 3, 2)]
+    zpeer = [device(zl + k, x, y) for k in (2, 1, 3)]
     xpeer = {k: device(zl, x + k, y) for k in (2, 1, 3)}
-    yfar = [device(zl, x, y + k) for k in (2, 6, 4)]
+    yfar = [device(zl, x, y + k) for k in (4, 2, 6)]
     yup, ydown = device(zl, x, y + 1), device(zl, x, y + NY - 1)
     mate = [device(zl, x, ymate, zh + a) for a in range(NH)]
     hpeer = [device(zl, x, y, zh + a) for a in (1, 2)]
@@ -54,7 +56,7 @@
         pltpu.make_async_copy(basis, basis_v, lsem.at[1]),
         pltpu.make_async_copy(grad.at[:, lo], ga.at[yh, zl], lsem.at[2]),
         pltpu.make_async_copy(grad.at[:, hi], gb.at[yh, zl], lsem.at[3]),
-        pltpu.make_async_copy(ob, bbuf.at[par, 0], lsem.at[4]),
+        pltpu.make_async_copy(ob, bbuf.at[par, XSLOT[0]], lsem.at[4]),
     ]
     for c in local:
         c.start()
@@ -77,13 +79,13 @@
         send(grad.at[:, lo], ga.at[yh, zl], garecv.at[yh, zl], d)
     for d in yfar:
         send(grad.at[:, hi], gb.at[yh, zl], gbrecv.at[yh, zl], d)
-    send(ob, bbuf.at[par, 0], brecv.at[par, 0], mate[0])
+    send(ob, bbuf.at[par, XSLOT[0]], brecv.at[par, 0], mate[0])
     for d in yfar:
         send(grad.at[:, lo], ga.at[yh, zl], garecv.at[yh, zl], d)
     for d in zpeer:
         send(grad.at[:, hi], gb.at[yh, zl], gbrecv.at[yh, zl], d)
     for k, d in xpeer.items():
-        send(ob, bbuf.at[par, NX - k], brecv.at[par, NX - k], d)
+        send(ob, bbuf.at[par, XSLOT[NX - k]], brecv.at[par, NX - k], d)
 
     local[0].wait()
     local[1].wait()
@@ -123,16 +125,16 @@
         landed(ga.at[yh, z_], garecv.at[yh, z_])
         for d in yfar:
             send(ga.at[yh, z_], ga.at[yh, z_], garecv.at[yh, z_], d)
+    other = 1 - par
+    landed(bbuf.at[other, XSLOT[0]], brecv.at[other, 0])
+    for k, d in xpeer.items():
+        send(bbuf.at[other, XSLOT[0]], bbuf.at[other, XSLOT[NX - k]], brecv.at[other, NX - k], d)
+
     hs = [(yh + k) % NP for k in (0, 1, 3, 2)]
     for h_ in hs[1:]:
         landed(gb.at[h_, zl], gbrecv.at[h_, zl])
         for d in zpeer:
             send(gb.at[h_, zl], gb.at[h_, zl], gbrecv.at[h_, zl], d)
-    other = 1 - par
-    landed(bbuf.at[other, 0], brecv.at[other, 0])
-    for k, d in xpeer.items():
-        send(bbuf.at[other, 0], bbuf.at[other, NX - k], brecv.at[other, NX - k], d)
-
     hop(0, zs[1:])
     hop(1)
     local[2].wait()
@@ -146,61 +148,73 @@
             landed(gb.at[h_, z_], gbrecv.at[h_, z_])
 
     for q in (other, par):
-        for k in (1, 3, 2):
-            landed(bbuf.at[q, k], brecv.at[q, k])
-        nt = (((1,), (1,)), ((), ()))
-        lhs = bbuf[q].reshape(NX * COLS, FEAT)
+        for k in (2, 1, 3):
+            landed(bbuf.at[q, XSLOT[k]], brecv.at[q, k])
+    nt = (((1,), (1,)), ((), ()))
+    groups = [(a, q) for a in range(NA) for q in (other, par)]
+    for a, q in groups:
+        lhs = bbuf[q, 2 * a : 2 * a + 2].reshape(2 * COLS, FEAT)
         p = lax.dot_general(lhs[:, :FH], ga[...].reshape(PTOK, FH), nt, preferred_element_type=F32)
         p = p + lax.dot_general(lhs[:, FH:], gb[...].reshape(PTOK, FH), nt, preferred_element_type=F32)
         p = p.reshape(NH, NC, SLICE, PTOK)
         for c in range(NC):
-            part[c, q] = p[:, c]
-        send(part.at[1 - core, q], sib_in.at[q], crecv.at[q], twin)
-    for q in (other, par):
-        landed(sib_in.at[q], crecv.at[q])
-        psum[q] = part[core, q] + sib_in[q]
+            part[c, a, q] = p[:, c]
+        send(part.at[1 - core, a, q], sib_in.at[a, q], crecv.at[a, q], twin)
+    for a, q in groups:
+        landed(sib_in.at[a, q], crecv.at[a, q])
+        psum[a, q] = part[core, a, q] + sib_in[a, q]
         for i, d in enumerate(hpeer):
-            send(psum.at[q, (zh + 1 + i) % NH], zin.at[q, 1 - i], zrecv.at[q, 1 - i], d)
+            send(psum.at[a, q, (zh + 1 + i) % NH], zin.at[a, q, 1 - i], zrecv.at[a, q, 1 - i], d)
     hop(2)
-    for q in (other, par):
-        acc = psum[q, zh]
+    for a, q in groups:
+        acc = psum[a, q, zh]
         for i in range(NH - 1):
-            landed(zin.at[q, i], zrecv.at[q, i])
-            acc = acc + zin[q, i]
+            landed(zin.at[a, q, i], zrecv.at[a, q, i])
+            acc = acc + zin[a, q, i]
         val = (acc * acc).astype(BF16)
         if q is other:
-            away[...] = val
+            away[a] = val
             for d in mate:
-                send(away, sq.at[par, tensor], qrecv.at[par, tensor], d)
+                send(away.at[a], sq.at[a, par, tensor], qrecv.at[a, par, tensor], d)
         else:
-            sq[par, tensor] = val
+            sq[a, par, tensor] = val
             for d in hpeer + [twin]:
-                send(sq.at[par, tensor], sq.at[par, tensor], qrecv.at[par, tensor], d)
+                send(sq.at[a, par, tensor], sq.at[a, par, tensor], qrecv.at[a, par, tensor], d)
     hop(3)
-    same = [((zh + a) % NH) * NC + core for a in range(NH)]
-    across = [((zh + a) % NH) * NC + 1 - core for a in range(NH)]
-    for q, js in ((other, same), (par, same[1:])):
-        for j in js:
-            landed(sq.at[q, j], qrecv.at[q, j])
-            send(sq.at[q, j], sq.at[q, j], qrecv.at[q, j], twin)
-    for z_ in zs:
-        landed(*slot((y + 4) % NY, z_))
-    for q in (other, par):
-        for j in across:
-            landed(sq.at[q, j], qrecv.at[q, j])
-
+    same = [((zh + b) % NH) * NC + core for b in range(NH)]
+    across = [((zh + b) % NH) * NC + 1 - core for b in range(NH)]
+
+    for a in range(NA):
+        for q, js in ((other, same), (par, same[1:])):
+            for j in js:
+                landed(sq.at[a, q, j], qrecv.at[a, q, j])
+                send(sq.at[a, q, j], sq.at[a, q, j], qrecv.at[a, q, j], twin)
+        if a == 0:
+            for z_ in zs:
+                landed(*slot((y + 4) % NY, z_))
+        for q in (other, par):
+            for j in across:
+                landed(sq.at[a, q, j], qrecv.at[a, q, j])
+        for n in range(2):
+            acc = None
+            for q in range(NQ):
+                rhs = sbuf[q, :, :, :, n * FH : (n + 1) * FH].reshape(PTOK, FH)
+                p = jnp.dot(sq[a, q].reshape(2 * COLS, PTOK), rhs, preferred_element_type=F32)
+                acc = p if acc is None else acc + p
+            eig[n, 2 * a : 2 * a + 2] = acc.reshape(2, COLS, FH)
+            if a == 0:
+                to = xpeer[1] if n == 0 else xpeer[3]
+                send(eig.at[n, XSLOT[2]], passing.at[n], precv.at[n], to)
+        if a == 1:
+            send(eig.at[1, XSLOT[1]], eig_in.at[1, 0], erecv.at[1, 0], xpeer[1])
+            send(eig.at[0, XSLOT[3]], eig_in.at[0, 0], erecv.at[0, 0], xpeer[3])
+    for n, k in ((0, 1), (1, 3)):
+        landed(passing.at[n], precv.at[n])
+        eig[n, XSLOT[k]] = eig[n, XSLOT[k]] + passing[n]
+        send(eig.at[n, XSLOT[k]], eig_in.at[n, 1], erecv.at[n, 1], xpeer[k])
     for n in range(2):
-        acc = None
-        for q in range(NQ):
-            rhs = sbuf[q, :, :, :, n * FH : (n + 1) * FH].reshape(PTOK, FH)
-            p = jnp.dot(sq[q].reshape(NX * COLS, PTOK), rhs, preferred_element_type=F32)
-            acc = p if acc is None else acc + p
-        eig[n] = acc.reshape(NX, COLS, FH)
-        for k, d in xpeer.items():
-            send(eig.at[n, k], eig_in.at[n, NX - k - 1], erecv.at[n, NX - k - 1], d)
-    for n in range(2):
-        acc = eig[n, 0]
-        for k in (0, 2, 1):
+        acc = eig[n, XSLOT[0]]
+        for k in range(2):
             landed(eig_in.at[n, k], erecv.at[n, k])
             acc = acc + eig_in[n, k]
         out[:, n * FH : (n + 1) * FH] = acc * F32(1.0 / TOKENS)
@@ -223,24 +237,26 @@
             pltpu.VMEM((NQ, NX, COLS, FEAT), BF16),
             pltpu.VMEM((TOK, FEAT), BF16),
             pltpu.VMEM((HEADS, HD, HD), BF16),
-            pltpu.VMEM((NC, NQ, NH, SLICE, PTOK), F32),
-            pltpu.VMEM((NQ, NH, SLICE, PTOK), F32),
-            pltpu.VMEM((NQ, NH, SLICE, PTOK), F32),
-            pltpu.VMEM((NQ, NH - 1, SLICE, PTOK), F32),
-            pltpu.VMEM((SLICE, PTOK), BF16),
-            pltpu.VMEM((NQ, NT, SLICE, PTOK), BF16),
+            pltpu.VMEM((NC, NA, NQ, NH, SLICE, PTOK), F32),
+            pltpu.VMEM((NA, NQ, NH, SLICE, PTOK), F32),
+            pltpu.VMEM((NA, NQ, NH, SLICE, PTOK), F32),
+            pltpu.VMEM((NA, NQ, NH - 1, SLICE, PTOK), F32),
+            pltpu.VMEM((NA, SLICE, PTOK), BF16),
+            pltpu.VMEM((NA, NQ, NT, SLICE, PTOK), BF16),
             pltpu.VMEM((2, NX, COLS, FH), F32),
-            pltpu.VMEM((2, NX - 1, COLS, FH), F32),
+            pltpu.VMEM((2, 2, COLS, FH), F32),
+            pltpu.VMEM((2, COLS, FH), F32),
             dma((5,)),
             dma((SENDS,)),
             dma((NP, NZ)),
             dma((NP, NZ)),
             dma((NY, NZ)),
             dma((NQ, NX)),
-            dma((NQ,)),
-            dma((NQ, NH - 1)),
-            dma((NQ, NT)),
-            dma((2, NX - 1)),
+            dma((NA, NQ)),
+            dma((NA, NQ, NH - 1)),
+            dma((NA, NQ, NT)),
+            dma((2, 2)),
+            dma((2,)),
         ],
         compiler_params=pltpu.CompilerParams(
             collective_id=0, has_side_effects=True, vmem_limit_bytes=24 << 20

time: 63.1 us -> 60.1 us (0.952)
  Pallas kernels: 62.2 us -> 59 us
    pallas_call x1, Pallas kernels: 62.2 us -> 59 us  [per_device(): pl.pallas_call(kernel, out_shape=jax.ShapeDtypeStruct((COLS, FEAT), F32),...]
where the time goes in v3:
time: 60.1 us; the launch traced here: 59.7 us
  Pallas kernels  59 us (98%)
  local copies, waits for them, and re-layouts  0.68 us (1%)
    pallas_call x1, Pallas kernels, per_device(): pl.pallas_call(kernel, out_shape=jax.ShapeDtypeStruct((COLS, FEAT), F32),...  59 us

profile of v3, /device:TPU:1, one launch (start us, length us, event | category | flops | bytes accessed | tf_op | source)
XLA Modules:
  0.0 59.7 jit_solution(2799470064581746042)
XLA Ops:
  0.0 59.0 %eigen_fit.1 = f32[48,1024]{1,0:T(8,128)S(1)} custom-call(bf16[16,1024]{1,0:T(8,128)(2,1)} %inp.1, bf16[8,128,128]{2,1,0:T(8,128)(2,1)} %basis.1, bf16[16,1024]{1,0:T(8,128)(2,1)} %grad.1, bf16[48,1024]{1,0:T(8,128)(2,1)} %bitcast.3), custom_call_target="tpu_custom_call" | custom-call | flops 400000000 | bytes 1000000 | tf_op jit(solution)/shard_map/eigen_fit/pallas_call | solution.py:228
  59.0 0.7 %copy.6 = f32[1024,48]{0,1:T(8,128)} copy(f32[1024,48]{0,1:T(8,128)S(1)} %bitcast.2) | data formatting | bytes 393216
